TPU v7x, 32 devices: a whole 2x2x4 slice. The times are simulated.
32 devices in a mesh: occ: 8 (over z, y), vir: 4 (over x, core).
Axes of the slice: x: 2, y: 2, z: 4, core: 2. Of those that a mesh axis runs over, the one named last changes fastest.
Arguments:
- factors: bfloat16 [2, 3072, 6144], P(None, 'occ', 'vir'), may hold values from -0.41992188 to 0.41992188
- occ_energy: float32 [2], replicated, may hold values from -1.2 to -0.4
- vir_energy: float32 [3072], replicated, may hold values from 0.4 to 2.5
- block_lengths: int32 [4, 8], replicated, may hold values from 1 to 512, 1536 in all within a row
- block_owner: int32 [4, 8], replicated, may hold values from 0 to 7, each once within a row
Outputs:
- gamma_owned: bfloat16 [16384, 2, 3072], P(('occ', 'vir'))
Inputs may be any that keep to these rules, and one draw needn't show every extreme that they name: `block_lengths`: each row sums to 1536, and every row's largest entry is exactly 512. `block_owner`: each row names every owner index once.
All inputs are finite; a program needn't handle non-finite values.
Results may differ from a plain program's by a relative error of at most 0.0037.
Values may be sent and summed in bfloat16 or wider, within the bound.
No kernel may reach another device: no remote copies, remote signals or barrier semaphores. Data moves between devices by JAX's collectives and lax.ppermute only.
A program may use at most 128 MiB of HBM per device.

v0:
```python
import jax
import jax.numpy as jnp
from jax import lax
from jax.sharding import PartitionSpec as P


def pair_terms(own_block, arrived):
    return jnp.einsum("iap,jbp->ijab", own_block, arrived, preferred_element_type=jnp.float32)


def amplitudes(pair_block, occupied_sum, near_energy, far_energy):
    denominator = (
        occupied_sum[:, :, None, None]
        - near_energy[None, None, :, None]
        - far_energy[None, None, None, :]
    )
    swapped = jnp.transpose(pair_block, (1, 0, 2, 3))
    return ((2.0 * pair_block - swapped) / denominator).astype(jnp.bfloat16)


def per_device(factors, occ_energy, vir_energy, block_lengths, block_owner):
    cycle_size = lax.axis_size("occ")
    cycle_index = lax.axis_index("occ")
    quarter_index = lax.axis_index("vir")
    occupied, tile_rows, quarter_width = factors.shape
    occupied_sum = occ_energy[:, None] + occ_energy[None, :]
    near_energy = lax.dynamic_slice_in_dim(vir_energy, cycle_index * tile_rows, tile_rows)
    every_tile = lax.all_gather(factors, "occ", axis=1, tiled=True)
    pair_block = pair_terms(factors, every_tile)
    summed = lax.psum(pair_block.reshape(-1), "vir").reshape(pair_block.shape)
    amplitude = amplitudes(summed, occupied_sum, near_energy, vir_energy)
    accum_gamma = jnp.einsum(
        "ijab,jbp->iap", amplitude, every_tile, preferred_element_type=jnp.float32
    )
    gamma_local = accum_gamma.astype(jnp.bfloat16)
    capacity = 8 * quarter_width // (3 * cycle_size)
    lengths_row = lax.dynamic_index_in_dim(block_lengths, quarter_index, 0, keepdims=False)
    owners_row = lax.dynamic_index_in_dim(block_owner, quarter_index, 0, keepdims=False)
    starts_row = jnp.cumsum(lengths_row) - lengths_row
    owner_match = owners_row[None, :] == jnp.arange(cycle_size, dtype=jnp.int32)[:, None]
    dest_start = jnp.sum(jnp.where(owner_match, starts_row[None, :], 0), axis=1)
    dest_length = jnp.sum(jnp.where(owner_match, lengths_row[None, :], 0), axis=1)
    slot_index = jnp.arange(capacity, dtype=jnp.int32)
    columns = jnp.minimum(dest_start[:, None] + slot_index[None, :], quarter_width - 1)
    live_slot = slot_index[None, :] < dest_length[:, None]
    by_column = jnp.transpose(gamma_local, (2, 0, 1))
    picked = jnp.take(by_column, columns.reshape(-1), axis=0)
    picked = jnp.where(live_slot.reshape(-1)[:, None, None], picked, jnp.zeros((), jnp.bfloat16))
    outgoing = picked.reshape(cycle_size, capacity * occupied * tile_rows)
    incoming = lax.all_to_all(outgoing, "occ", split_axis=0, concat_axis=0, tiled=True)
    incoming = incoming.reshape(cycle_size, capacity, occupied, tile_rows)
    return jnp.transpose(incoming, (1, 2, 0, 3)).reshape(capacity, occupied, cycle_size * tile_rows)


def solution(mesh):
    placed = (P(None, "occ", "vir"), P(), P(), P(), P())
    return jax.shard_map(
        per_device,
        mesh=mesh,
        in_specs=placed,
        out_specs=P(("occ", "vir"), None, None),
        check_vma=False,
    )
```

profile of v0, /device:TPU:26, one launch (start us, length us, event | category | flops | bytes accessed | tf_op | source)
XLA Modules:
  0.0 1116.9 jit_solution(18100837095018694897)
XLA Ops:
  6.5 0.0 all-gather.2.cloned.1.call-start
  6.5 0.7 all-gather.2.cloned.1.call-update
  7.3 0.0 all-reduce.2.cloned.1.call-start
  7.3 365.0 %all-gather.2.cloned.1.call-done = bf16[2,3072,1536]{2,1,0:T(8,128)(2,1)} async-done(((bf16[2,384,1536]{2,1,0:T(8,128)(2,1)}), bf16[2,3072,1536]{2,1,0:T(8,128)(2,1)}) %all-gather.2.cloned.1.call-update) | async-done | bytes 18874384 | tf_op jit(solution)/shard_map/all_gather | solution.py:28
  372.3 20.9 %fusion.10 = f32[2,2,384,3072]{2,3,0,1:T(8,128)} fusion(bf16[2,3072,1536]{2,1,0:T(8,128)(2,1)} %all-gather.2.cloned.1.call-done, bf16[2,384,1536]{2,1,0:T(8,128)(2,1)} %param.5), kind=kOutput, calls=%fused_computation.14 | convolution fusion | flops 14495514624 | bytes 40108032 | tf_op jit(solution)/shard_map/iap,jbp->ijab/dot_general | solution.py:8
  393.3 0.0 copy-start.2
  393.3 0.0 copy-start.1
  393.3 0.0 copy-start
  393.3 0.0 all-reduce.2.cloned.1.call-update
  393.3 0.6 copy-done.2
  394.0 0.2 reduce-window_clone.1
  394.1 0.7 subtract_bitcast_fusion
  394.8 0.1 select_reduce_fusion
  395.0 0.1 fusion.25
  395.1 0.1 fusion.24
  395.2 0.0 copy-done.1
  395.2 0.1 dynamic_slice.12
  395.3 0.0 copy-done
  395.3 0.1 broadcast_add_fusion
  395.4 0.1 broadcast_subtract_fusion
  395.5 319.0 %all-reduce.2.cloned.1.call-done = f32[2,2,384,3072]{2,3,0,1:T(8,128)} async-done(((f32[2,2,384,3072]{2,3,0,1:T(8,128)}), f32[2,2,384,3072]{2,3,0,1:T(8,128)}) %all-reduce.2.cloned.1.call-update) | async-done | bytes 18874384 | tf_op jit(solution)/shard_map/psum | solution.py:30
  714.5 28.2 %fusion.17 = bf16[1536,2,384]{0,2,1:T(8,128)(2,1)} fusion(bf16[2,3072,1536]{2,1,0:T(8,128)(2,1)} %all-gather.2.cloned.1.call-done, f32[2,2,384,3072]{2,3,0,1:T(8,128)} %all-reduce.2.cloned.1.call-done, f32[3072]{0:T(1024)S(1)} %copy-done.1, f32[2,2,384]{2,1,0:T(2,128)S(1)} %broadcast_subtract_fusion), kind=kOutput, calls=%fused_computation.16 | convolution fusion | flops 14520287232 | bytes 40126464 | tf_op jit(solution)/shard_map/ijab,jbp->iap/dot_general | solution.py:32
  742.7 6.6 copy.24
  749.3 37.0 %gather_fusion = bf16[4096,2,384]{2,1,0:T(2,128)(2,1)} fusion(bf16[1536,2,384]{2,1,0:T(2,128)(2,1)S(1)} %copy.24, s32[4096]{0:T(1024)S(1)} %broadcast_clamp_fusion), kind=kCustom, calls=%fused_computation | custom fusion | bytes 12599296 | tf_op jit(solution)/shard_map/jit(_take)/gather | solution.py:47
  786.3 24.8 %broadcast_select_fusion.1 = bf16[4096,2,384]{2,1,0:T(2,128)(2,1)} fusion(pred[4096]{0:T(1024)(128)(4,1)S(1)} %bitcast.61, bf16[4096,2,384]{2,1,0:T(2,128)(2,1)} %gather_fusion, pred[4096]{0:T(1024)(128)(4,1)S(1)} %compare_and_fusion), kind=kLoop, calls=%fused_computation.10 | loop fusion | flops 6291456 | bytes 12591104 | tf_op jit(solution)/shard_map/jit(_where)/select_n | solution.py:48
  811.1 10.6 select_n.68
  821.7 0.5 broadcast.106
  822.3 40.3 %reduce.1 = bf16[8,393216]{1,0:T(8,128)(2,1)} reduce(bf16[8,1,393216]{2,1,0:T(2,128)(2,1)} %select_n.68, bf16[]{:T(256)} %broadcast.106), dimensions={1}, to_apply=%select_n.68.reduce_sub_computation | reduce | bytes 12582914 | tf_op jit(solution)/shard_map/jit(_where)/select_n | solution.py:48
  862.6 11.4 %reshape.170 = bf16[8,2,196608]{2,1,0:T(2,128)(2,1)} reshape(bf16[8,393216]{1,0:T(8,128)(2,1)} %reduce.1) | data formatting | bytes 12582912
  874.0 141.7 %all_to_all.6 = bf16[8,2,196608]{2,1,0:T(2,128)(2,1)} all-to-all(bf16[8,2,196608]{2,1,0:T(2,128)(2,1)} %reshape.170), channel_id=1, replica_groups=mesh['occ'=8,'vir'=4] {'occ'}, dimensions={0} | all-to-all | bytes 12582912 | tf_op jit(solution)/shard_map/all_to_all | solution.py:50
  1015.7 10.9 reshape.171
  1026.7 39.5 %reduce = bf16[8,393216]{1,0:T(8,128)(2,1)} reduce(bf16[8,1,393216]{2,1,0:T(2,128)(2,1)} %reshape.171, bf16[]{:T(256)} %constant.45), dimensions={1}, to_apply=%all_to_all.4.reduce_sub_computation | reduce | bytes 12582914 | tf_op jit(solution)/shard_map/all_to_all | solution.py:50
  1066.2 11.4 %reshape.155 = bf16[8,512,2,384]{3,2,1,0:T(2,128)(2,1)} reshape(bf16[8,393216]{1,0:T(8,128)(2,1)} %reduce) | data formatting | bytes 12582912 | tf_op jit(solution)/shard_map/reshape | solution.py:51
  1077.6 16.1 %copy.26 = bf16[512,2,8,384]{0,3,2,1:T(8,128)(2,1)} copy(bf16[512,2,8,384]{3,1,0,2:T(2,128)(2,1)} %bitcast.56) | data formatting | bytes 12582912 | tf_op jit(solution)/shard_map/transpose | solution.py:52
  1093.7 16.3 %copy.27 = bf16[512,2,3072]{2,1,0:T(2,128)(2,1)} copy(bf16[512,2,3072]{0,2,1:T(8,128)(2,1)} %bitcast.57) | data formatting | bytes 12582912 | tf_op jit(solution)/shard_map/reshape | solution.py:52
  (8 shorter events, 0.1 us)
Async XLA Ops:
  6.5 365.8 %all-gather.2.cloned.1.call-start = ((), (), s32[]{:S(2)}) async-start(), calls=%async_computation.1 | async-start | bytes 21233664 | tf_op jit(solution)/shard_map/all_gather | solution.py:28
  7.3 707.3 %all-reduce.2.cloned.1.call-start = ((), (), s32[]{:S(2)}) async-start(), calls=%async_computation.2 | async-start | bytes 37748736 | tf_op jit(solution)/shard_map/psum | solution.py:30
  393.3 0.7 copy-start.2
  393.3 1.9 copy-start.1
  393.3 2.0 copy-start
Sparse Core Ops, SparseCore 0:
  8.9 363.3 all-gather.1
  393.4 321.0 all-reduce.1
where the time goes:
time: 1120 us
  waiting for transfers between devices  685 us (61%)
  blocking collectives  142 us (13%)
  local copies, waits for them, and re-layouts  122 us (11%)
  other arithmetic  106 us (9%)
  matrix products  49.2 us (4%)
  between operations  13.5 us (1%)
    all_gather x1, waiting for transfers between devices, per_device(): every_tile = lax.all_gather(factors, 'occ', axis=1, tiled=True)  365 us
    psum x1, waiting for transfers between devices, per_device(): summed = lax.psum(pair_block.reshape(-1), 'vir').reshape(pair_block.shape)  319 us
    all_to_all x1, blocking collectives, per_device(): lax.all_to_all(outgoing, 'occ', split_axis=0, concat_axis=0, tiled=True)  142 us
    select_n x2, other arithmetic, per_device(): jnp.where(live_slot.reshape(-1)[:, None, None], picked, jnp.zeros((), jnp...  65.1 us
    all_to_all x1, other arithmetic, per_device(): lax.all_to_all(outgoing, 'occ', split_axis=0, concat_axis=0, tiled=True)  39.5 us
    gather x1, local copies, waits for them, and re-layouts, per_device(): picked = jnp.take(by_column, columns.reshape(-1), axis=0)  37 us
    dot_general x1, matrix products, per_device(): jnp.einsum('ijab,jbp->iap', amplitude, every_tile, preferred_element_type...  28.2 us
    unnamed x11, local copies, waits for them, and re-layouts  23.1 us
  transfers between devices with their start and end apart: 2, of which 2 were waited for; matrix products, arithmetic and copies ran while one was open for 0% of the time, Pallas kernels for 0%

commit v1 on v0

v1 whole, which is shorter than its diff:
```python
import jax
import jax.numpy as jnp
from jax import lax
from jax.sharding import PartitionSpec as P


def grid_cycle(places):
    spans = [sorted({p[d] for p in places}) for d in range(len(places[0]))]
    order = sorted(range(len(spans)), key=lambda d: -len(spans[d]))
    grid = {}
    for index, p in enumerate(places):
        grid[tuple(spans[d].index(p[d]) for d in order)] = index
    sizes = [len(spans[d]) for d in order]

    def snake(dims):
        if not dims:
            return [()]
        inner, out = snake(dims[1:]), []
        for k in range(dims[0]):
            out += [(k,) + rest for rest in (inner if k % 2 == 0 else inner[::-1])]
        return out

    rest = snake(sizes[1:])
    walk = [(k,) + rest[0] for k in range(sizes[0])]
    for back, k in enumerate(reversed(range(sizes[0]))):
        line = rest[1:]
        walk += [(k,) + r for r in (line if back % 2 == 0 else line[::-1])]
    return [grid[w] for w in walk]


def choose(marks, array):
    return lax.dot_general(marks, array, (((1,), (1,)), ((), ())), preferred_element_type=jnp.float32).astype(
        jnp.bfloat16
    )


def solution(mesh):
    cycle_size, groups = mesh.shape["occ"], mesh.shape["vir"]
    places = [tuple(row[0].coords) for row in mesh.devices.reshape(cycle_size, groups)]
    cycle = grid_cycle(places)
    position_of = [cycle.index(k) for k in range(cycle_size)]
    long_axis = max(range(3), key=lambda d: len({p[d] for p in places}))
    levels = sorted({p[long_axis] for p in places})
    planes = [[k for k in range(cycle_size) if places[k][long_axis] == level] for level in levels]
    heights, members = len(planes), len(planes[0])
    plane_of = [levels.index(p[long_axis]) for p in places]
    member_of = [planes[plane_of[k]].index(k) for k in range(cycle_size)]
    unrolled = cycle_size <= 16

    def pairs_of(target):
        return [(k * groups + v, target(k) * groups + v) for k in range(cycle_size) for v in range(groups)]

    def along_cycle(shift):
        return pairs_of(lambda k: cycle[(position_of[k] + shift) % cycle_size])

    def along_planes(shift):
        return pairs_of(lambda k: planes[(plane_of[k] + shift) % heights][member_of[k]])

    def along_members(shift):
        return pairs_of(lambda k: planes[plane_of[k]][(member_of[k] + shift) % members])

    def across_groups(bit):
        return [(k * groups + v, k * groups + (v ^ bit)) for k in range(cycle_size) for v in range(groups)]

    def send(array, pairs):
        return lax.ppermute(array, ("occ", "vir"), pairs)

    ahead, behind, core = along_cycle(1), along_cycle(-1), across_groups(1)
    wider = [across_groups(1 << bit) for bit in range(1, groups.bit_length() - 1)]

    def per_device(factors, occ_energy, vir_energy, block_lengths, block_owner):
        me, group = lax.axis_index("occ"), lax.axis_index("vir")
        occupied, tile_rows, width = factors.shape
        capacity = 8 * width // (3 * cycle_size)
        lanes = 2 if unrolled else 1
        part = tile_rows // (2 * lanes)
        even = group % 2 == 0
        occupied_sum = occ_energy[:, None] + occ_energy[None, :]

        def of_me(table):
            return lax.dynamic_index_in_dim(jnp.array(table, jnp.int32), me, 0, keepdims=False)

        def shard_at(step):
            return of_me([cycle[(position_of[k] + step) % cycle_size] for k in range(cycle_size)])

        tiles = vir_energy.reshape(cycle_size, tile_rows)
        near = lax.dynamic_index_in_dim(tiles, me, 0, keepdims=False)

        def term_of(lane, low, high, low_far, high_far):
            low_at, high_at = lane * part, (lanes + lane) * part
            mine, other = jnp.where(even, low, high), jnp.where(even, high, low)
            far = jnp.where(even, low_far[low_at : low_at + part], high_far[high_at : high_at + part])
            def pair(block):
                return jnp.einsum("iap,jbp->ijab", factors, block, preferred_element_type=jnp.float32)

            total = pair(mine) + send(pair(other), core)
            for pairs in wider:
                total = total + send(total.astype(jnp.bfloat16), pairs).astype(jnp.float32)
            denominator = (
                occupied_sum[:, :, None, None] - near[None, None, :, None] - far[None, None, None, :]
            )
            t = ((2.0 * total - jnp.transpose(total, (1, 0, 2, 3))) / denominator).astype(jnp.bfloat16)
            return [t, send(t, core)], [mine, other]

        def term(lows, highs, low_far, high_far):
            amplitude, blocks = [], []
            for lane in range(lanes):
                t, b = term_of(lane, lows[lane], highs[lane], low_far, high_far)
                amplitude, blocks = amplitude + t, blocks + b
            return jnp.einsum(
                "ijab,jbp->iap",
                jnp.concatenate(amplitude, axis=3),
                jnp.concatenate(blocks, axis=1),
                preferred_element_type=jnp.float32,
            )

        lengths = lax.dynamic_index_in_dim(block_lengths, group, 0, keepdims=False)
        owners = lax.dynamic_index_in_dim(block_owner, group, 0, keepdims=False)
        starts = jnp.cumsum(lengths) - lengths
        ordered = jnp.array([k for plane in planes for k in plane], jnp.int32)
        match = owners[None, :] == ordered[:, None]
        own_start = jnp.sum(jnp.where(match, starts[None, :], 0), axis=1)
        own_length = jnp.sum(jnp.where(match, lengths[None, :], 0), axis=1)

        lows = [factors[:, k * part : (k + 1) * part] for k in range(lanes)]
        highs = [factors[:, (lanes + k) * part : (lanes + k + 1) * part] for k in range(lanes)]
        if unrolled:
            gammas = []
            for step in range(cycle_size):
                if step >= 4:
                    lows, highs, gammas[step - 4] = lax.optimization_barrier((lows, highs, gammas[step - 4]))
                if step + 1 < cycle_size:
                    next_lows = [send(x, ahead) for x in lows]
                    next_highs = [send(x, behind) for x in highs]
                low_far = lax.dynamic_index_in_dim(tiles, shard_at(-step), 0, keepdims=False)
                high_far = lax.dynamic_index_in_dim(tiles, shard_at(step), 0, keepdims=False)
                new = term(lows, highs, low_far, high_far)
                gammas.append(new if step == 0 else gammas[-1] + new)
                lows, highs = next_lows, next_highs
            gamma = gammas[-1]
        else:
            cycle_table = jnp.array(cycle + cycle, jnp.int32)
            place = of_me(position_of)

            def one_step(step, carry):
                lows, highs, gamma = carry
                lows, highs = [send(x, ahead) for x in lows], [send(x, behind) for x in highs]
                low_far = lax.dynamic_index_in_dim(tiles, cycle_table[place + cycle_size - step], 0, keepdims=False)
                high_far = lax.dynamic_index_in_dim(tiles, cycle_table[place + step], 0, keepdims=False)
                return lows, highs, gamma + term(lows, highs, low_far, high_far)

            first = term(lows, highs, near, near)
            gamma = lax.fori_loop(1, cycle_size, one_step, (lows, highs, first))[2]
        gamma = gamma.astype(jnp.bfloat16).reshape(occupied * tile_rows, width)
        column = jnp.arange(width, dtype=jnp.int32)[None, :]
        slot = jnp.arange(capacity, dtype=jnp.int32)

        def columns_at(start, length):
            return jnp.where(slot < length, start + slot, -1)

        if not unrolled:
            wanted = jnp.where(slot[None, :] < own_length[:, None], own_start[:, None] + slot[None, :], -1)
            outgoing = choose((wanted.reshape(-1, 1) == column).astype(jnp.bfloat16), gamma)
            outgoing = outgoing.reshape(cycle_size, capacity, occupied * tile_rows)
            inverse = [ordered_at for plane in planes for ordered_at in plane]
            outgoing = jnp.stack([outgoing[inverse.index(k)] for k in range(cycle_size)])
            incoming = lax.all_to_all(outgoing, "occ", split_axis=0, concat_axis=0, tiled=True)
            incoming = incoming.reshape(cycle_size, capacity, occupied, tile_rows)
            return jnp.transpose(incoming, (1, 2, 0, 3)).reshape(capacity, occupied, cycle_size * tile_rows)

        plane_at, member_at = of_me(plane_of), of_me(member_of)
        every_match = block_owner[:, None, :] == ordered[None, :, None]
        every_length = jnp.sum(jnp.where(every_match, block_lengths[:, None, :], 0), axis=2)
        fullest = jnp.max(jnp.sum(every_length.reshape(groups, heights, members), axis=2))
        own_start, own_length = own_start.reshape(heights, members), own_length.reshape(heights, members)
        twice_start = jnp.concatenate([own_start, own_start])
        twice_length = jnp.concatenate([own_length, own_length])
        plane_start = lax.dynamic_slice_in_dim(twice_start, plane_at, heights)
        plane_length = lax.dynamic_slice_in_dim(twice_length, plane_at, heights)
        my_length = plane_length[0]
        turned = (jnp.arange(members)[:, None] + member_at) % members == jnp.arange(members)[None, :]
        turned_length = jnp.sum(jnp.where(turned, my_length[None, :], 0), axis=1)
        turned_offset = jnp.sum(jnp.where(turned, (jnp.cumsum(my_length) - my_length)[None, :], 0), axis=1)
        turned_start = jnp.sum(jnp.where(turned, plane_start[0][None, :], 0), axis=1)

        def exchange(room):
            def run(gamma):
                wide = jnp.arange(room, dtype=jnp.int32)
                wide_column = wide[None, :]
                result = jnp.zeros((capacity, occupied, cycle_size * tile_rows), jnp.bfloat16)
                for rise in range(heights):
                    if rise:
                        wanted = jnp.full((room,), -1, jnp.int32)
                        at = jnp.zeros((), jnp.int32)
                        for m in range(members):
                            length = plane_length[rise, m]
                            here = (wide >= at) & (wide < at + length)
                            wanted = jnp.where(here, plane_start[rise, m] + wide - at, wanted)
                            at = at + length
                        packed = choose((wanted[:, None] == column).astype(jnp.bfloat16), gamma)
                        packed = send(packed, along_planes(rise))
                    for turn in range(members):
                        if rise:
                            wanted = jnp.where(slot < turned_length[turn], turned_offset[turn] + slot, -1)
                            marks = (wanted[:, None] == wide_column).astype(jnp.bfloat16)
                            piece = jnp.dot(marks, packed, preferred_element_type=jnp.float32).astype(jnp.bfloat16)
                        else:
                            wanted = columns_at(turned_start[turn], turned_length[turn])
                            piece = choose((wanted[:, None] == column).astype(jnp.bfloat16), gamma)
                        if turn:
                            piece = send(piece, along_members(turn))
                        source = of_me(
                            [
                                planes[(plane_of[k] - rise) % heights][(member_of[k] - turn) % members]
                                for k in range(cycle_size)
                            ]
                        )
                        piece = piece.reshape(capacity, occupied, tile_rows)
                        result = lax.dynamic_update_slice_in_dim(result, piece, source * tile_rows, 2)
                return result

            return run

        rooms = list(range(capacity, members * capacity + 1, capacity // 8))
        which = jnp.sum((fullest > jnp.array(rooms, jnp.int32)).astype(jnp.int32))
        return lax.switch(which, [exchange(room) for room in rooms], gamma)

    placed = (P(None, "occ", "vir"), P(), P(), P(), P())
    return jax.shard_map(
        per_device,
        mesh=mesh,
        in_specs=placed,
        out_specs=P(("occ", "vir"), None, None),
        check_vma=False,
    )
```

time: 1120 us -> 534 us (0.48)
  waiting for transfers between devices: 685 us -> 230 us
  blocking collectives: 142 us -> 0 us
  other arithmetic: 106 us -> 36.2 us
  local copies, waits for them, and re-layouts: 122 us -> 54.2 us
  starting transfers between devices: 0.04 us -> 53.9 us
  matrix products: 49.2 us -> 97.5 us
  loops' own time: 0 us -> 43.5 us
    all_gather x1 -> x0, waiting for transfers between devices: 365 us -> none  [per_device(): every_tile = lax.all_gather(factors, 'occ', axis=1, tiled=True)]
    psum x1 -> x0, waiting for transfers between devices: 319 us -> none  [per_device(): summed = lax.psum(pair_block.reshape(-1), 'vir').reshape(pair_block.shape)]
    ppermute x0 -> x83, waiting for transfers between devices: none -> 230 us  [send(): return lax.ppermute(array, ('occ', 'vir'), pairs)]
    all_to_all x1 -> x0, blocking collectives: 142 us -> none  [per_device(): lax.all_to_all(outgoing, 'occ', split_axis=0, concat_axis=0, tiled=True)]
    ppermute x0 -> x83, starting transfers between devices: none -> 53.9 us  [send(): return lax.ppermute(array, ('occ', 'vir'), pairs)]
    dot_general x2 -> x51, matrix products: 49.2 us -> 97.5 us  [the longest x32 33.9 us: pair(): jnp.einsum('iap,jbp->ijab', factors, block, preferred_element_type=jnp.fl...]
    select_n x3 -> x24, other arithmetic: 65.1 us -> 18.3 us  [the longest x15 6.93 us: term_of(): mine, other = (jnp.where(even, low, high), jnp.where(even, high, low))]
    another operation x0 -> x1, loops' own time: none -> 43.5 us  [per_device(): return lax.switch(which, [exchange(room) for room in rooms], gamma)]
  transfers between devices with their start and end apart: 2 -> 83, of which waited for: 2 -> 32; matrix products, arithmetic and copies ran while one was open for 0% -> 31% of each run, Pallas kernels for 0% -> 0%
where the time goes in v1:
time: 534 us
  waiting for transfers between devices  230 us (43%)
  matrix products  97.5 us (18%)
  local copies, waits for them, and re-layouts  54.2 us (10%)
  starting transfers between devices  53.9 us (10%)
  loops' own time  43.5 us (8%)
  other arithmetic  36.2 us (7%)
  between operations  18.6 us (3%)
    ppermute x83, waiting for transfers between devices, send(): return lax.ppermute(array, ('occ', 'vir'), pairs)  230 us
    ppermute x83, starting transfers between devices, send(): return lax.ppermute(array, ('occ', 'vir'), pairs)  53.9 us
    another operation x1, loops' own time, per_device(): return lax.switch(which, [exchange(room) for room in rooms], gamma)  43.5 us
    dot_general x32, matrix products, pair(): jnp.einsum('iap,jbp->ijab', factors, block, preferred_element_type=jnp.fl...  33.9 us
    dot_general x8, matrix products, term(): jnp.einsum('ijab,jbp->iap', jnp.concatenate(amplitude, axis=3), jnp.conca...  28.8 us
    dot_general x6, matrix products, run(): jnp.dot(marks, packed, preferred_element_type=jnp.float32)  17.8 us
    dot_general x5, matrix products, choose(): lax.dot_general(marks, array, (((1,), (1,)), ((), ())), preferred_element...  17 us
    dynamic_slice x17, local copies, waits for them, and re-layouts, of_me(): lax.dynamic_index_in_dim(jnp.array(table, jnp.int32), me, 0, keepdims=False)  16.4 us
  transfers between devices with their start and end apart: 83, of which 32 were waited for; matrix products, arithmetic and copies ran while one was open for 31% of the time, Pallas kernels for 0%

profile of v1, /device:TPU:26, one launch (start us, length us, event | category | flops | bytes accessed | tf_op | source)
XLA Modules:
  0.0 533.5 jit_solution(4994231529528864832)
XLA Ops:
  0.0 3.3 broadcast_select_fusion.31
  5.3 1.8 fusion.617
  7.1 1.7 fusion.599
  51.4 2.0 fusion.884
  53.4 2.0 fusion.882
  59.4 2.0 fusion.941
  62.0 2.0 fusion.940
  67.0 4.9 collective-permute-done.69
  74.6 2.6 collective-permute-done.64
  77.9 5.4 %collective-permute-done.84 = bf16[2,96,1536]{2,1,0:T(8,128)(2,1)S(1)} collective-permute-done((bf16[2,96,1536]{2,1,0:T(8,128)(2,1)}, bf16[2,96,1536]{2,1,0:T(8,128)(2,1)S(1)}, u32[]{:S(2)}, u32[]{:S(2)}) %collective-permute-start.84) | collective-permute-done | bytes 589856 | tf_op jit(solution)/shard_map/ppermute | solution.py:66
  84.9 3.5 collective-permute-done.85
  94.1 4.2 convolution_bitcast_fusion
  101.9 5.9 %collective-permute-done.72 = bf16[2,2,384,96]{2,3,1,0:T(8,128)(2,1)S(1)} collective-permute-done((bf16[2,2,384,96]{2,3,1,0:T(8,128)(2,1)S(1)}, bf16[2,2,384,96]{2,3,1,0:T(8,128)(2,1)S(1)}, u32[]{:S(2)}, u32[]{:S(2)}) %collective-permute-start.72) | collective-permute-done | bytes 294944 | tf_op jit(solution)/shard_map/ppermute | solution.py:66
  109.1 4.4 collective-permute-done.94
  118.8 8.6 %collective-permute-done.90 = bf16[2,96,1536]{2,1,0:T(8,128)(2,1)S(1)} collective-permute-done((bf16[2,96,1536]{2,1,0:T(8,128)(2,1)S(1)}, bf16[2,96,1536]{2,1,0:T(8,128)(2,1)S(1)}, u32[]{:S(2)}, u32[]{:S(2)}) %collective-permute-start.90) | collective-permute-done | bytes 589856 | tf_op jit(solution)/shard_map/ppermute | solution.py:66
  134.8 8.9 %collective-permute-done.100 = bf16[2,96,1536]{2,1,0:T(8,128)(2,1)S(1)} collective-permute-done((bf16[2,96,1536]{2,1,0:T(8,128)(2,1)S(1)}, bf16[2,96,1536]{2,1,0:T(8,128)(2,1)S(1)}, u32[]{:S(2)}, u32[]{:S(2)}) %collective-permute-start.100) | collective-permute-done | bytes 589856 | tf_op jit(solution)/shard_map/ppermute | solution.py:66
  145.7 9.5 %collective-permute-done.102 = bf16[2,96,1536]{2,1,0:T(8,128)(2,1)S(1)} collective-permute-done((bf16[2,96,1536]{2,1,0:T(8,128)(2,1)S(1)}, bf16[2,96,1536]{2,1,0:T(8,128)(2,1)S(1)}, u32[]{:S(2)}, u32[]{:S(2)}) %collective-permute-start.102) | collective-permute-done | bytes 589856 | tf_op jit(solution)/shard_map/ppermute | solution.py:66
  160.5 2.4 collective-permute-done.97
  164.9 1.9 fusion.949
  169.2 6.3 %collective-permute-done.104 = bf16[2,2,384,96]{2,3,1,0:T(8,128)(2,1)S(1)} collective-permute-done((bf16[2,2,384,96]{2,3,1,0:T(8,128)(2,1)S(1)}, bf16[2,2,384,96]{2,3,1,0:T(8,128)(2,1)S(1)}, u32[]{:S(2)}, u32[]{:S(2)}) %collective-permute-start.104) | collective-permute-done | bytes 294944 | tf_op jit(solution)/shard_map/ppermute | solution.py:66
  175.5 1.9 fusion.822
  184.8 5.7 %bitcast_add_fusion.6 = f32[2,384,1536]{2,1,0:T(8,128)S(1)} fusion(f32[2,384,1536]{2,1,0:T(8,128)} %convolution_bitcast_fusion, bf16[2,96,1536]{2,1,0:T(8,128)(2,1)} %copy-done.28, bf16[2,96,1536]{2,1,0:T(8,128)(2,1)} %copy-done.10, bf16[2,96,1536]{2,1,0:T(8,128)(2,1)} %copy-done.31, bf16[2,96,1536]{2,1,0:T(8,128)(2,1)} %copy-done.13, ...), kind=kOutput, calls=%fused_computation.727 | convolution fusion | flops 1827274752 | bytes 12976128 | tf_op jit(solution)/shard_map/ijab,jbp->iap/dot_general | solution.py:110
  190.5 5.2 collective-permute-done.109
  195.8 12.2 %collective-permute-done.110 = bf16[2,96,1536]{2,1,0:T(8,128)(2,1)S(1)} collective-permute-done((bf16[2,96,1536]{2,1,0:T(8,128)(2,1)}, bf16[2,96,1536]{2,1,0:T(8,128)(2,1)S(1)}, u32[]{:S(2)}, u32[]{:S(2)}) %collective-permute-start.110) | collective-permute-done | bytes 589856 | tf_op jit(solution)/shard_map/ppermute | solution.py:66
  211.7 2.1 bitcast_add_fusion.5
  216.4 2.2 bitcast_add_fusion.4
  219.6 16.9 %collective-permute-done.119 = bf16[2,96,1536]{2,1,0:T(8,128)(2,1)S(1)} collective-permute-done((bf16[2,96,1536]{2,1,0:T(8,128)(2,1)S(1)}, bf16[2,96,1536]{2,1,0:T(8,128)(2,1)S(1)}, u32[]{:S(2)}, u32[]{:S(2)}) %collective-permute-start.119) | collective-permute-done | bytes 589856 | tf_op jit(solution)/shard_map/ppermute | solution.py:66
  245.2 7.0 %collective-permute-done.117 = bf16[2,2,384,96]{2,3,1,0:T(8,128)(2,1)S(1)} collective-permute-done((bf16[2,2,384,96]{2,3,1,0:T(8,128)(2,1)S(1)}, bf16[2,2,384,96]{2,3,1,0:T(8,128)(2,1)S(1)}, u32[]{:S(2)}, u32[]{:S(2)}) %collective-permute-start.117) | collective-permute-done | bytes 294944 | tf_op jit(solution)/shard_map/ppermute | solution.py:66
  253.0 12.0 %collective-permute-done.130 = bf16[2,96,1536]{2,1,0:T(8,128)(2,1)S(1)} collective-permute-done((bf16[2,96,1536]{2,1,0:T(8,128)(2,1)S(1)}, bf16[2,96,1536]{2,1,0:T(8,128)(2,1)S(1)}, u32[]{:S(2)}, u32[]{:S(2)}) %collective-permute-start.130) | collective-permute-done | bytes 589856 | tf_op jit(solution)/shard_map/ppermute | solution.py:66
  268.1 2.0 collective-permute-start.127
  272.3 10.0 %collective-permute-done.127 = bf16[2,2,384,96]{2,3,1,0:T(8,128)(2,1)S(1)} collective-permute-done((bf16[2,2,384,96]{2,3,1,0:T(8,128)(2,1)S(1)}, bf16[2,2,384,96]{2,3,1,0:T(8,128)(2,1)S(1)}, u32[]{:S(2)}, u32[]{:S(2)}) %collective-permute-start.127) | collective-permute-done | bytes 294944 | tf_op jit(solution)/shard_map/ppermute | solution.py:66
  282.4 4.6 collective-permute-done.124
  291.3 2.1 fusion.502
  293.4 1.8 collective-permute-start.134
  295.2 2.1 fusion.509
  297.3 3.5 collective-permute-done.137
  300.9 5.8 %collective-permute-done.134 = bf16[2,2,384,96]{2,3,0,1:T(8,128)(2,1)S(1)} collective-permute-done((bf16[2,2,384,96]{2,3,0,1:T(8,128)(2,1)S(1)}, bf16[2,2,384,96]{2,3,0,1:T(8,128)(2,1)S(1)}, u32[]{:S(2)}, u32[]{:S(2)}) %collective-permute-start.134) | collective-permute-done | bytes 294944 | tf_op jit(solution)/shard_map/ppermute | solution.py:66
  307.6 4.2 fusion.516
  311.9 6.3 %fusion.477 = bf16[2,384,1536]{2,1,0:T(8,128)(2,1)} fusion(f32[2,384,1536,1]{2,1,0,3:T(8,128)} %fusion.516, f32[2,384,1536,1]{2,1,0,3:T(8,128)S(1)} %fusion.509, f32[2,384,1536]{2,1,0:T(8,128)S(1)} %bitcast_add_fusion.4, f32[2,384,1536,1]{2,1,0,3:T(8,128)S(1)} %fusion.502, bf16[2,96,1536]{2,1,0:T(8,128)(2,1)S(1)} %get-tuple-element.2743, ...), kind=kOutput, calls=%fused_computation.721 | convolution fusion | flops 1831993344 | bytes 24772608 | tf_op jit(solution)/shard_map/ijab,jbp->iap/dot_general | solution.py:110
  318.2 214.0 %conditional.1 = (bf16[512,2,3072]{2,1,0:T(2,128)(2,1)}) conditional(s32[]{:T(128)} %clamp.3, (s32[2]{0:T(128)S(1)}, s32[512]{0:T(512)S(1)}, s32[2,2]{1,0:T(2,128)S(1)}, s32[512]{0:T(512)S(1)}, s32[1,1536]{1,0:T(1,128)S(1)}, /*index=5*/s32[1,1536]{1,0:T(1,128)S(1)}, s32[1,1536]{1,0:T(1,128)S(1)}, ...), branch_computations={%region_11.12_spmd, %region_12.13_spmd, %region_13.14_spmd, %regio... | conditional | flops 14510489600 | bytes 104753560 | solution.py:226
  346.8 4.2 fusion.344
  354.0 1.8 select_select_fusion.20
  355.8 3.5 fusion.328
  359.4 2.1 collective-permute-start.43
  362.8 1.8 select_select_fusion.19
  364.6 3.5 fusion.331
  369.8 1.9 select_select_fusion.18
  371.8 3.5 fusion.334
  387.8 2.3 fusion.341
  390.1 2.3 reshape.1095
  392.4 5.9 %broadcast.1008 = bf16[512,2,3072]{2,1,0:T(2,128)(2,1)} broadcast(bf16[]{:T(256)} %constant.474.clone), dimensions={} | broadcast | bytes 6291458 | tf_op jit(solution)/shard_map/broadcast.44
  401.4 3.3 fusion.350
  404.6 1.9 collective-permute-start.44
  406.6 74.1 %collective-permute-done.45 = bf16[896,768]{1,0:T(8,128)(2,1)} collective-permute-done((bf16[896,768]{1,0:T(8,128)(2,1)}, bf16[896,768]{1,0:T(8,128)(2,1)}, u32[]{:S(2)}, u32[]{:S(2)}) %collective-permute-start.45) | collective-permute-done | bytes 1376288 | tf_op jit(solution)/shard_map/cond/branch_6_fun/ppermute | solution.py:66
  480.6 3.3 fusion.351
  484.8 3.3 fusion.352
  489.2 2.4 fusion.347
  491.6 2.4 fusion.348
  494.0 3.3 fusion.349
  497.6 2.5 reshape.1101
  501.5 2.1 reshape.1098
  504.7 2.1 reshape.1100
  512.4 7.0 %collective-permute-done.48 = bf16[512,768]{1,0:T(8,128)(2,1)} collective-permute-done((bf16[512,768]{1,0:T(8,128)(2,1)}, bf16[512,768]{1,0:T(8,128)(2,1)}, u32[]{:S(2)}, u32[]{:S(2)}) %collective-permute-start.48) | collective-permute-done | bytes 786464 | tf_op jit(solution)/shard_map/cond/branch_6_fun/ppermute | solution.py:66
  519.4 2.1 reshape.1102
  (392 shorter events, 138.6 us)
Async XLA Ops:
  3.3 52.1 %collective-permute-start.74 = (bf16[2,96,1536]{2,1,0:T(8,128)(2,1)}, bf16[2,96,1536]{2,1,0:T(8,128)(2,1)}, u32[]{:S(2)}, u32[]{:S(2)}) collective-permute-start(bf16[2,96,1536]{2,1,0:T(8,128)(2,1)} %get-tuple-element.2736), channel_id=1, source_target_pairs={{0,8},{1,9},{2,10},{3,11},{4,0},{5,1},{6,2},{7,3},{8,16},{9,17},{1... | collective-permute-start | bytes 1769480 | tf_op jit(solution)/shard_map/ppermute | solution.py:66
  4.8 52.2 %collective-permute-start.75 = (bf16[2,96,1536]{2,1,0:T(8,128)(2,1)}, bf16[2,96,1536]{2,1,0:T(8,128)(2,1)}, u32[]{:S(2)}, u32[]{:S(2)}) collective-permute-start(bf16[2,96,1536]{2,1,0:T(8,128)(2,1)} %get-tuple-element.2735), channel_id=1, source_target_pairs={{0,4},{1,5},{2,6},{3,7},{4,12},{5,13},{6,14},{7,15},{8,0},{9,1},{1... | collective-permute-start | bytes 1769480 | tf_op jit(solution)/shard_map/ppermute | solution.py:66
  7.1 52.3 %collective-permute-start.66 = (f32[2,2,384,96]{2,3,1,0:T(8,128)}, f32[2,2,384,96]{2,3,1,0:T(8,128)}, u32[]{:S(2)}, u32[]{:S(2)}) collective-permute-start(f32[2,2,384,96]{2,3,1,0:T(8,128)} %fusion.617), channel_id=1, source_target_pairs={{0,1},{1,0},{2,3},{3,2},{4,5},{5,4},{6,7},{7,6},{8,9},{9,8},{10,11... | collective-permute-start | bytes 1769480 | tf_op jit(solution)/shard_map/ppermute | solution.py:66
  8.9 53.1 %collective-permute-start.63 = (f32[2,2,384,96]{2,3,0,1:T(8,128)}, f32[2,2,384,96]{2,3,0,1:T(8,128)}, u32[]{:S(2)}, u32[]{:S(2)}) collective-permute-start(f32[2,2,384,96]{2,3,0,1:T(8,128)} %fusion.599), channel_id=1, source_target_pairs={{0,1},{1,0},{2,3},{3,2},{4,5},{5,4},{6,7},{7,6},{8,9},{9,8},{10,11... | collective-permute-start | bytes 1769480 | tf_op jit(solution)/shard_map/ppermute | solution.py:66
  9.4 56.1 %collective-permute-start.70 = (bf16[2,96,1536]{2,1,0:T(8,128)(2,1)}, bf16[2,96,1536]{2,1,0:T(8,128)(2,1)}, u32[]{:S(2)}, u32[]{:S(2)}) collective-permute-start(bf16[2,96,1536]{2,1,0:T(8,128)(2,1)} %get-tuple-element.2733), channel_id=1, source_target_pairs={{0,4},{1,5},{2,6},{3,7},{4,12},{5,13},{6,14},{7,15},{8,0},{9,1},{1... | collective-permute-start | bytes 1769480 | tf_op jit(solution)/shard_map/ppermute | solution.py:66
  55.4 16.5 %collective-permute-start.69 = (bf16[2,96,1536]{2,1,0:T(8,128)(2,1)}, bf16[2,96,1536]{2,1,0:T(8,128)(2,1)S(1)}, u32[]{:S(2)}, u32[]{:S(2)}) collective-permute-start(bf16[2,96,1536]{2,1,0:T(8,128)(2,1)} %get-tuple-element.2734), channel_id=1, source_target_pairs={{0,8},{1,9},{2,10},{3,11},{4,0},{5,1},{6,2},{7,3},{8,16},{9,17},{1... | collective-permute-start | bytes 1769480 | tf_op jit(solution)/shard_map/ppermute | solution.py:66
  59.3 30.1 %collective-permute-start.76 = (f32[2,2,384,96]{2,3,1,0:T(8,128)S(1)}, f32[2,2,384,96]{2,3,1,0:T(8,128)S(1)}, u32[]{:S(2)}, u32[]{:S(2)}) collective-permute-start(f32[2,2,384,96]{2,3,1,0:T(8,128)S(1)} %fusion.635), channel_id=1, source_target_pairs={{0,1},{1,0},{2,3},{3,2},{4,5},{5,4},{6,7},{7,6},{8,9},{9,8},{10,11... | collective-permute-start | bytes 1769480 | tf_op jit(solution)/shard_map/ppermute | solution.py:66
  61.4 13.1 %collective-permute-start.67 = (bf16[2,2,384,96]{2,3,1,0:T(8,128)(2,1)S(1)}, bf16[2,2,384,96]{2,3,1,0:T(8,128)(2,1)S(1)}, u32[]{:S(2)}, u32[]{:S(2)}) collective-permute-start(bf16[2,2,384,96]{2,3,1,0:T(8,128)(2,1)S(1)} %get-tuple-element.2801), channel_id=1, source_target_pairs={{0,2},{1,3},{2,0},{3,1},{4,6},{5,7},{6,4},{7,5},{8,10},{9,11},{10,... | collective-permute-start | bytes 884744 | tf_op jit(solution)/shard_map/ppermute | solution.py:66
  63.9 13.2 %collective-permute-start.64 = (bf16[2,2,384,96]{2,3,0,1:T(8,128)(2,1)S(1)}, bf16[2,2,384,96]{2,3,0,1:T(8,128)(2,1)S(1)}, u32[]{:S(2)}, u32[]{:S(2)}) collective-permute-start(bf16[2,2,384,96]{2,3,0,1:T(8,128)(2,1)S(1)} %get-tuple-element.2799), channel_id=1, source_target_pairs={{0,2},{1,3},{2,0},{3,1},{4,6},{5,7},{6,4},{7,5},{8,10},{9,11},{10,... | collective-permute-start | bytes 884744 | tf_op jit(solution)/shard_map/ppermute | solution.py:66
  65.5 17.8 %collective-permute-start.84 = (bf16[2,96,1536]{2,1,0:T(8,128)(2,1)}, bf16[2,96,1536]{2,1,0:T(8,128)(2,1)S(1)}, u32[]{:S(2)}, u32[]{:S(2)}) collective-permute-start(bf16[2,96,1536]{2,1,0:T(8,128)(2,1)} %collective-permute-done.74), channel_id=1, source_target_pairs={{0,8},{1,9},{2,10},{3,11},{4,0},{5,1},{6,2},{7,3},{8,16},{9,17},{1... | collective-permute-start | bytes 1769480 | tf_op jit(solution)/shard_map/ppermute | solution.py:66
  71.9 16.5 %collective-permute-start.85 = (bf16[2,96,1536]{2,1,0:T(8,128)(2,1)}, bf16[2,96,1536]{2,1,0:T(8,128)(2,1)S(1)}, u32[]{:S(2)}, u32[]{:S(2)}) collective-permute-start(bf16[2,96,1536]{2,1,0:T(8,128)(2,1)} %collective-permute-done.75), channel_id=1, source_target_pairs={{0,4},{1,5},{2,6},{3,7},{4,12},{5,13},{6,14},{7,15},{8,0},{9,1},{1... | collective-permute-start | bytes 1769480 | tf_op jit(solution)/shard_map/ppermute | solution.py:66
  74.4 16.5 %collective-permute-start.71 = (f32[2,2,384,96]{2,3,1,0:T(8,128)S(1)}, f32[2,2,384,96]{2,3,1,0:T(8,128)S(1)}, u32[]{:S(2)}, u32[]{:S(2)}) collective-permute-start(f32[2,2,384,96]{2,3,1,0:T(8,128)S(1)} %fusion.626), channel_id=1, source_target_pairs={{0,1},{1,0},{2,3},{3,2},{4,5},{5,4},{6,7},{7,6},{8,9},{9,8},{10,11... | collective-permute-start | bytes 1769480 | tf_op jit(solution)/shard_map/ppermute | solution.py:66
  77.2 21.1 %collective-permute-start.80 = (bf16[2,96,1536]{2,1,0:T(8,128)(2,1)}, bf16[2,96,1536]{2,1,0:T(8,128)(2,1)S(1)}, u32[]{:S(2)}, u32[]{:S(2)}) collective-permute-start(bf16[2,96,1536]{2,1,0:T(8,128)(2,1)} %collective-permute-done.70), channel_id=1, source_target_pairs={{0,4},{1,5},{2,6},{3,7},{4,12},{5,13},{6,14},{7,15},{8,0},{9,1},{1... | collective-permute-start | bytes 1769480 | tf_op jit(solution)/shard_map/ppermute | solution.py:66
  83.3 16.6 %collective-permute-start.79 = (bf16[2,96,1536]{2,1,0:T(8,128)(2,1)S(1)}, bf16[2,96,1536]{2,1,0:T(8,128)(2,1)S(1)}, u32[]{:S(2)}, u32[]{:S(2)}) collective-permute-start(bf16[2,96,1536]{2,1,0:T(8,128)(2,1)S(1)} %collective-permute-done.69), channel_id=1, source_target_pairs={{0,8},{1,9},{2,10},{3,11},{4,0},{5,1},{6,2},{7,3},{8,16},{9,17},{1... | collective-permute-start | bytes 1769480 | tf_op jit(solution)/shard_map/ppermute | solution.py:66
  90.9 26.4 %collective-permute-start.86 = (f32[2,2,384,96]{2,3,1,0:T(8,128)S(1)}, f32[2,2,384,96]{2,3,1,0:T(8,128)S(1)}, u32[]{:S(2)}, u32[]{:S(2)}) collective-permute-start(f32[2,2,384,96]{2,3,1,0:T(8,128)S(1)} %fusion.653), channel_id=1, source_target_pairs={{0,1},{1,0},{2,3},{3,2},{4,5},{5,4},{6,7},{7,6},{8,9},{9,8},{10,11... | collective-permute-start | bytes 1769480 | tf_op jit(solution)/shard_map/ppermute | solution.py:66
  92.6 15.2 %collective-permute-start.72 = (bf16[2,2,384,96]{2,3,1,0:T(8,128)(2,1)S(1)}, bf16[2,2,384,96]{2,3,1,0:T(8,128)(2,1)S(1)}, u32[]{:S(2)}, u32[]{:S(2)}) collective-permute-start(bf16[2,2,384,96]{2,3,1,0:T(8,128)(2,1)S(1)} %get-tuple-element.2815), channel_id=1, source_target_pairs={{0,2},{1,3},{2,0},{3,1},{4,6},{5,7},{6,4},{7,5},{8,10},{9,11},{10,... | collective-permute-start | bytes 884744 | tf_op jit(solution)/shard_map/ppermute | solution.py:66
  98.3 15.2 %collective-permute-start.94 = (bf16[2,96,1536]{2,1,0:T(8,128)(2,1)S(1)}, bf16[2,96,1536]{2,1,0:T(8,128)(2,1)S(1)}, u32[]{:S(2)}, u32[]{:S(2)}) collective-permute-start(bf16[2,96,1536]{2,1,0:T(8,128)(2,1)S(1)} %collective-permute-done.84), channel_id=1, source_target_pairs={{0,8},{1,9},{2,10},{3,11},{4,0},{5,1},{6,2},{7,3},{8,16},{9,17},{1... | collective-permute-start | bytes 1769480 | tf_op jit(solution)/shard_map/ppermute | solution.py:66
  99.9 16.2 %collective-permute-start.95 = (bf16[2,96,1536]{2,1,0:T(8,128)(2,1)S(1)}, bf16[2,96,1536]{2,1,0:T(8,128)(2,1)S(1)}, u32[]{:S(2)}, u32[]{:S(2)}) collective-permute-start(bf16[2,96,1536]{2,1,0:T(8,128)(2,1)S(1)} %collective-permute-done.85), channel_id=1, source_target_pairs={{0,4},{1,5},{2,6},{3,7},{4,12},{5,13},{6,14},{7,15},{8,0},{9,1},{1... | collective-permute-start | bytes 1769480 | tf_op jit(solution)/shard_map/ppermute | solution.py:66
  101.8 27.7 %collective-permute-start.81 = (f32[2,2,384,96]{2,3,1,0:T(8,128)S(1)}, f32[2,2,384,96]{2,3,1,0:T(8,128)S(1)}, u32[]{:S(2)}, u32[]{:S(2)}) collective-permute-start(f32[2,2,384,96]{2,3,1,0:T(8,128)S(1)} %fusion.644), channel_id=1, source_target_pairs={{0,1},{1,0},{2,3},{3,2},{4,5},{5,4},{6,7},{7,6},{8,9},{9,8},{10,11... | collective-permute-start | bytes 1769480 | tf_op jit(solution)/shard_map/ppermute | solution.py:66
  107.7 19.7 %collective-permute-start.90 = (bf16[2,96,1536]{2,1,0:T(8,128)(2,1)S(1)}, bf16[2,96,1536]{2,1,0:T(8,128)(2,1)S(1)}, u32[]{:S(2)}, u32[]{:S(2)}) collective-permute-start(bf16[2,96,1536]{2,1,0:T(8,128)(2,1)S(1)} %collective-permute-done.80), channel_id=1, source_target_pairs={{0,4},{1,5},{2,6},{3,7},{4,12},{5,13},{6,14},{7,15},{8,0},{9,1},{1... | collective-permute-start | bytes 1769480 | tf_op jit(solution)/shard_map/ppermute | solution.py:66
  113.5 15.5 %collective-permute-start.89 = (bf16[2,96,1536]{2,1,0:T(8,128)(2,1)S(1)}, bf16[2,96,1536]{2,1,0:T(8,128)(2,1)S(1)}, u32[]{:S(2)}, u32[]{:S(2)}) collective-permute-start(bf16[2,96,1536]{2,1,0:T(8,128)(2,1)S(1)} %collective-permute-done.79), channel_id=1, source_target_pairs={{0,8},{1,9},{2,10},{3,11},{4,0},{5,1},{6,2},{7,3},{8,16},{9,17},{1... | collective-permute-start | bytes 1769480 | tf_op jit(solution)/shard_map/ppermute | solution.py:66
  117.2 16.5 %collective-permute-start.96 = (f32[2,2,384,96]{2,3,1,0:T(8,128)S(1)}, f32[2,2,384,96]{2,3,1,0:T(8,128)S(1)}, u32[]{:S(2)}, u32[]{:S(2)}) collective-permute-start(f32[2,2,384,96]{2,3,1,0:T(8,128)S(1)} %fusion.671), channel_id=1, source_target_pairs={{0,1},{1,0},{2,3},{3,2},{4,5},{5,4},{6,7},{7,6},{8,9},{9,8},{10,11... | collective-permute-start | bytes 1769480 | tf_op jit(solution)/shard_map/ppermute | solution.py:66
  118.2 13.8 %collective-permute-start.87 = (bf16[2,2,384,96]{2,3,1,0:T(8,128)(2,1)S(1)}, bf16[2,2,384,96]{2,3,1,0:T(8,128)(2,1)S(1)}, u32[]{:S(2)}, u32[]{:S(2)}) collective-permute-start(bf16[2,2,384,96]{2,3,1,0:T(8,128)(2,1)S(1)} %get-tuple-element.2809), channel_id=1, source_target_pairs={{0,2},{1,3},{2,0},{3,1},{4,6},{5,7},{6,4},{7,5},{8,10},{9,11},{10,... | collective-permute-start | bytes 884744 | tf_op jit(solution)/shard_map/ppermute | solution.py:66
  127.4 16.3 %collective-permute-start.100 = (bf16[2,96,1536]{2,1,0:T(8,128)(2,1)S(1)}, bf16[2,96,1536]{2,1,0:T(8,128)(2,1)S(1)}, u32[]{:S(2)}, u32[]{:S(2)}) collective-permute-start(bf16[2,96,1536]{2,1,0:T(8,128)(2,1)S(1)} %collective-permute-done.94), channel_id=1, source_target_pairs={{0,8},{1,9},{2,10},{3,11},{4,0},{5,1},{6,2},{7,3},{8,16},{9,17},{1... | collective-permute-start | bytes 1769480 | tf_op jit(solution)/shard_map/ppermute | solution.py:66
  128.9 16.3 %collective-permute-start.101 = (bf16[2,96,1536]{2,1,0:T(8,128)(2,1)S(1)}, bf16[2,96,1536]{2,1,0:T(8,128)(2,1)S(1)}, u32[]{:S(2)}, u32[]{:S(2)}) collective-permute-start(bf16[2,96,1536]{2,1,0:T(8,128)(2,1)S(1)} %collective-permute-done.90), channel_id=1, source_target_pairs={{0,4},{1,5},{2,6},{3,7},{4,12},{5,13},{6,14},{7,15},{8,0},{9,1},{1... | collective-permute-start | bytes 1769480 | tf_op jit(solution)/shard_map/ppermute | solution.py:66
  129.5 25.7 %collective-permute-start.102 = (bf16[2,96,1536]{2,1,0:T(8,128)(2,1)S(1)}, bf16[2,96,1536]{2,1,0:T(8,128)(2,1)S(1)}, u32[]{:S(2)}, u32[]{:S(2)}) collective-permute-start(bf16[2,96,1536]{2,1,0:T(8,128)(2,1)S(1)} %collective-permute-done.95), channel_id=1, source_target_pairs={{0,4},{1,5},{2,6},{3,7},{4,12},{5,13},{6,14},{7,15},{8,0},{9,1},{1... | collective-permute-start | bytes 1769480 | tf_op jit(solution)/shard_map/ppermute | solution.py:66
  132.1 23.8 %collective-permute-start.99 = (bf16[2,96,1536]{2,1,0:T(8,128)(2,1)S(1)}, bf16[2,96,1536]{2,1,0:T(8,128)(2,1)S(1)}, u32[]{:S(2)}, u32[]{:S(2)}) collective-permute-start(bf16[2,96,1536]{2,1,0:T(8,128)(2,1)S(1)} %collective-permute-done.89), channel_id=1, source_target_pairs={{0,8},{1,9},{2,10},{3,11},{4,0},{5,1},{6,2},{7,3},{8,16},{9,17},{1... | collective-permute-start | bytes 1769480 | tf_op jit(solution)/shard_map/ppermute | solution.py:66
  133.8 49.3 %collective-permute-start.73 = (bf16[2,2,384,96]{2,3,0,1:T(8,128)(2,1)}, bf16[2,2,384,96]{2,3,0,1:T(8,128)(2,1)}, u32[]{:S(2)}, u32[]{:S(2)}) collective-permute-start(bf16[2,2,384,96]{2,3,0,1:T(8,128)(2,1)} %fusion.846), channel_id=1, source_target_pairs={{0,1},{1,0},{2,3},{3,2},{4,5},{5,4},{6,7},{7,6},{8,9},{9,8},{10,11... | collective-permute-start | bytes 884744 | tf_op jit(solution)/shard_map/ppermute | solution.py:66
  143.7 13.3 %collective-permute-start.91 = (f32[2,2,384,96]{2,3,1,0:T(8,128)S(1)}, f32[2,2,384,96]{2,3,1,0:T(8,128)S(1)}, u32[]{:S(2)}, u32[]{:S(2)}) collective-permute-start(f32[2,2,384,96]{2,3,1,0:T(8,128)S(1)} %fusion.662), channel_id=1, source_target_pairs={{0,1},{1,0},{2,3},{3,2},{4,5},{5,4},{6,7},{7,6},{8,9},{9,8},{10,11... | collective-permute-start | bytes 1769480 | tf_op jit(solution)/shard_map/ppermute | solution.py:66
  145.2 22.6 %collective-permute-start.82 = (bf16[2,2,384,96]{2,3,1,0:T(8,128)(2,1)S(1)}, bf16[2,2,384,96]{2,3,1,0:T(8,128)(2,1)S(1)}, u32[]{:S(2)}, u32[]{:S(2)}) collective-permute-start(bf16[2,2,384,96]{2,3,1,0:T(8,128)(2,1)S(1)} %get-tuple-element.2807), channel_id=1, source_target_pairs={{0,2},{1,3},{2,0},{3,1},{4,6},{5,7},{6,4},{7,5},{8,10},{9,11},{10,... | collective-permute-start | bytes 884744 | tf_op jit(solution)/shard_map/ppermute | solution.py:66
  157.9 11.2 %collective-permute-start.92 = (bf16[2,2,384,96]{2,3,1,0:T(8,128)(2,1)S(1)}, bf16[2,2,384,96]{2,3,1,0:T(8,128)(2,1)S(1)}, u32[]{:S(2)}, u32[]{:S(2)}) collective-permute-start(bf16[2,2,384,96]{2,3,1,0:T(8,128)(2,1)S(1)} %get-tuple-element.2811), channel_id=1, source_target_pairs={{0,2},{1,3},{2,0},{3,1},{4,6},{5,7},{6,4},{7,5},{8,10},{9,11},{10,... | collective-permute-start | bytes 884744 | tf_op jit(solution)/shard_map/ppermute | solution.py:66
  163.9 11.6 %collective-permute-start.104 = (bf16[2,2,384,96]{2,3,1,0:T(8,128)(2,1)S(1)}, bf16[2,2,384,96]{2,3,1,0:T(8,128)(2,1)S(1)}, u32[]{:S(2)}, u32[]{:S(2)}) collective-permute-start(bf16[2,2,384,96]{2,3,1,0:T(8,128)(2,1)S(1)} %get-tuple-element.2803), channel_id=1, source_target_pairs={{0,2},{1,3},{2,0},{3,1},{4,6},{5,7},{6,4},{7,5},{8,10},{9,11},{10,... | collective-permute-start | bytes 884744 | tf_op jit(solution)/shard_map/ppermute | solution.py:66
  166.7 14.3 %collective-permute-start.107 = (bf16[2,2,384,96]{2,3,1,0:T(8,128)(2,1)}, bf16[2,2,384,96]{2,3,1,0:T(8,128)(2,1)}, u32[]{:S(2)}, u32[]{:S(2)}) collective-permute-start(bf16[2,2,384,96]{2,3,1,0:T(8,128)(2,1)} %get-tuple-element.2817), channel_id=1, source_target_pairs={{0,2},{1,3},{2,0},{3,1},{4,6},{5,7},{6,4},{7,5},{8,10},{9,11},{10,... | collective-permute-start | bytes 884744 | tf_op jit(solution)/shard_map/ppermute | solution.py:66
  179.4 16.4 %collective-permute-start.109 = (bf16[2,96,1536]{2,1,0:T(8,128)(2,1)}, bf16[2,96,1536]{2,1,0:T(8,128)(2,1)S(1)}, u32[]{:S(2)}, u32[]{:S(2)}) collective-permute-start(bf16[2,96,1536]{2,1,0:T(8,128)(2,1)} %copy-done.41), channel_id=1, source_target_pairs={{0,8},{1,9},{2,10},{3,11},{4,0},{5,1},{6,2},{7,3},{8,16},{9,17},{1... | collective-permute-start | bytes 1769480 | tf_op jit(solution)/shard_map/ppermute | solution.py:66
  179.9 28.1 %collective-permute-start.110 = (bf16[2,96,1536]{2,1,0:T(8,128)(2,1)}, bf16[2,96,1536]{2,1,0:T(8,128)(2,1)S(1)}, u32[]{:S(2)}, u32[]{:S(2)}) collective-permute-start(bf16[2,96,1536]{2,1,0:T(8,128)(2,1)} %copy-done.38), channel_id=1, source_target_pairs={{0,8},{1,9},{2,10},{3,11},{4,0},{5,1},{6,2},{7,3},{8,16},{9,17},{1... | collective-permute-start | bytes 1769480 | tf_op jit(solution)/shard_map/ppermute | solution.py:66
  181.1 27.0 %collective-permute-start.111 = (bf16[2,96,1536]{2,1,0:T(8,128)(2,1)}, bf16[2,96,1536]{2,1,0:T(8,128)(2,1)S(1)}, u32[]{:S(2)}, u32[]{:S(2)}) collective-permute-start(bf16[2,96,1536]{2,1,0:T(8,128)(2,1)} %copy-done.39), channel_id=1, source_target_pairs={{0,4},{1,5},{2,6},{3,7},{4,12},{5,13},{6,14},{7,15},{8,0},{9,1},{1... | collective-permute-start | bytes 1769480 | tf_op jit(solution)/shard_map/ppermute | solution.py:66
  183.1 26.0 %collective-permute-start.112 = (bf16[2,96,1536]{2,1,0:T(8,128)(2,1)}, bf16[2,96,1536]{2,1,0:T(8,128)(2,1)S(1)}, u32[]{:S(2)}, u32[]{:S(2)}) collective-permute-start(bf16[2,96,1536]{2,1,0:T(8,128)(2,1)} %copy-done.40), channel_id=1, source_target_pairs={{0,4},{1,5},{2,6},{3,7},{4,12},{5,13},{6,14},{7,15},{8,0},{9,1},{1... | collective-permute-start | bytes 1769480 | tf_op jit(solution)/shard_map/ppermute | solution.py:66
  184.8 24.9 %collective-permute-start.83 = (bf16[2,2,384,96]{2,3,0,1:T(8,128)(2,1)}, bf16[2,2,384,96]{2,3,0,1:T(8,128)(2,1)S(1)}, u32[]{:S(2)}, u32[]{:S(2)}) collective-permute-start(bf16[2,2,384,96]{2,3,0,1:T(8,128)(2,1)} %get-tuple-element.2788), channel_id=1, source_target_pairs={{0,1},{1,0},{2,3},{3,2},{4,5},{5,4},{6,7},{7,6},{8,9},{9,8},{10,11... | collective-permute-start | bytes 884744 | tf_op jit(solution)/shard_map/ppermute | solution.py:66
  195.8 15.5 %collective-permute-start.88 = (bf16[2,2,384,96]{2,3,0,1:T(8,128)(2,1)S(1)}, bf16[2,2,384,96]{2,3,0,1:T(8,128)(2,1)S(1)}, u32[]{:S(2)}, u32[]{:S(2)}) collective-permute-start(bf16[2,2,384,96]{2,3,0,1:T(8,128)(2,1)S(1)} %copy-done.46), channel_id=1, source_target_pairs={{0,1},{1,0},{2,3},{3,2},{4,5},{5,4},{6,7},{7,6},{8,9},{9,8},{10,11... | collective-permute-start | bytes 884744 | tf_op jit(solution)/shard_map/ppermute | solution.py:66
  209.1 27.4 %collective-permute-start.120 = (bf16[2,96,1536]{2,1,0:T(8,128)(2,1)S(1)}, bf16[2,96,1536]{2,1,0:T(8,128)(2,1)S(1)}, u32[]{:S(2)}, u32[]{:S(2)}) collective-permute-start(bf16[2,96,1536]{2,1,0:T(8,128)(2,1)S(1)} %collective-permute-done.110), channel_id=1, source_target_pairs={{0,8},{1,9},{2,10},{3,11},{4,0},{5,1},{6,2},{7,3},{8,16},{9,17},{1... | collective-permute-start | bytes 1769480 | tf_op jit(solution)/shard_map/ppermute | solution.py:66
  209.6 27.2 %collective-permute-start.122 = (bf16[2,96,1536]{2,1,0:T(8,128)(2,1)S(1)}, bf16[2,96,1536]{2,1,0:T(8,128)(2,1)S(1)}, u32[]{:S(2)}, u32[]{:S(2)}) collective-permute-start(bf16[2,96,1536]{2,1,0:T(8,128)(2,1)S(1)} %collective-permute-done.112), channel_id=1, source_target_pairs={{0,4},{1,5},{2,6},{3,7},{4,12},{5,13},{6,14},{7,15},{8,0},{9,1},{1... | collective-permute-start | bytes 1769480 | tf_op jit(solution)/shard_map/ppermute | solution.py:66
  211.2 25.2 %collective-permute-start.119 = (bf16[2,96,1536]{2,1,0:T(8,128)(2,1)S(1)}, bf16[2,96,1536]{2,1,0:T(8,128)(2,1)S(1)}, u32[]{:S(2)}, u32[]{:S(2)}) collective-permute-start(bf16[2,96,1536]{2,1,0:T(8,128)(2,1)S(1)} %collective-permute-done.109), channel_id=1, source_target_pairs={{0,8},{1,9},{2,10},{3,11},{4,0},{5,1},{6,2},{7,3},{8,16},{9,17},{1... | collective-permute-start | bytes 1769480 | tf_op jit(solution)/shard_map/ppermute | solution.py:66
  214.8 22.0 %collective-permute-start.121 = (bf16[2,96,1536]{2,1,0:T(8,128)(2,1)S(1)}, bf16[2,96,1536]{2,1,0:T(8,128)(2,1)S(1)}, u32[]{:S(2)}, u32[]{:S(2)}) collective-permute-start(bf16[2,96,1536]{2,1,0:T(8,128)(2,1)S(1)} %collective-permute-done.111), channel_id=1, source_target_pairs={{0,4},{1,5},{2,6},{3,7},{4,12},{5,13},{6,14},{7,15},{8,0},{9,1},{1... | collective-permute-start | bytes 1769480 | tf_op jit(solution)/shard_map/ppermute | solution.py:66
  216.4 23.7 %collective-permute-start.116 = (f32[2,2,384,96]{2,3,1,0:T(8,128)S(1)}, f32[2,2,384,96]{2,3,1,0:T(8,128)S(1)}, u32[]{:S(2)}, u32[]{:S(2)}) collective-permute-start(f32[2,2,384,96]{2,3,1,0:T(8,128)S(1)} %fusion.707), channel_id=1, source_target_pairs={{0,1},{1,0},{2,3},{3,2},{4,5},{5,4},{6,7},{7,6},{8,9},{9,8},{10,11... | collective-permute-start | bytes 1769480 | tf_op jit(solution)/shard_map/ppermute | solution.py:66
  236.8 16.2 %collective-permute-start.129 = (bf16[2,96,1536]{2,1,0:T(8,128)(2,1)S(1)}, bf16[2,96,1536]{2,1,0:T(8,128)(2,1)S(1)}, u32[]{:S(2)}, u32[]{:S(2)}) collective-permute-start(bf16[2,96,1536]{2,1,0:T(8,128)(2,1)S(1)} %collective-permute-done.119), channel_id=1, source_target_pairs={{0,8},{1,9},{2,10},{3,11},{4,0},{5,1},{6,2},{7,3},{8,16},{9,17},{1... | collective-permute-start | bytes 1769480 | tf_op jit(solution)/shard_map/ppermute | solution.py:66
  238.0 27.0 %collective-permute-start.130 = (bf16[2,96,1536]{2,1,0:T(8,128)(2,1)S(1)}, bf16[2,96,1536]{2,1,0:T(8,128)(2,1)S(1)}, u32[]{:S(2)}, u32[]{:S(2)}) collective-permute-start(bf16[2,96,1536]{2,1,0:T(8,128)(2,1)S(1)} %collective-permute-done.120), channel_id=1, source_target_pairs={{0,8},{1,9},{2,10},{3,11},{4,0},{5,1},{6,2},{7,3},{8,16},{9,17},{1... | collective-permute-start | bytes 1769480 | tf_op jit(solution)/shard_map/ppermute | solution.py:66
  238.4 27.7 %collective-permute-start.132 = (bf16[2,96,1536]{2,1,0:T(8,128)(2,1)S(1)}, bf16[2,96,1536]{2,1,0:T(8,128)(2,1)S(1)}, u32[]{:S(2)}, u32[]{:S(2)}) collective-permute-start(bf16[2,96,1536]{2,1,0:T(8,128)(2,1)S(1)} %collective-permute-done.122), channel_id=1, source_target_pairs={{0,4},{1,5},{2,6},{3,7},{4,12},{5,13},{6,14},{7,15},{8,0},{9,1},{1... | collective-permute-start | bytes 1769480 | tf_op jit(solution)/shard_map/ppermute | solution.py:66
  240.1 25.9 %collective-permute-start.131 = (bf16[2,96,1536]{2,1,0:T(8,128)(2,1)S(1)}, bf16[2,96,1536]{2,1,0:T(8,128)(2,1)S(1)}, u32[]{:S(2)}, u32[]{:S(2)}) collective-permute-start(bf16[2,96,1536]{2,1,0:T(8,128)(2,1)S(1)} %collective-permute-done.121), channel_id=1, source_target_pairs={{0,4},{1,5},{2,6},{3,7},{4,12},{5,13},{6,14},{7,15},{8,0},{9,1},{1... | collective-permute-start | bytes 1769480 | tf_op jit(solution)/shard_map/ppermute | solution.py:66
  252.2 38.6 %collective-permute-start.105 = (bf16[2,2,384,96]{2,3,0,1:T(8,128)(2,1)S(1)}, bf16[2,2,384,96]{2,3,0,1:T(8,128)(2,1)S(1)}, u32[]{:S(2)}, u32[]{:S(2)}) collective-permute-start(bf16[2,2,384,96]{2,3,0,1:T(8,128)(2,1)S(1)} %copy-done.42), channel_id=1, source_target_pairs={{0,1},{1,0},{2,3},{3,2},{4,5},{5,4},{6,7},{7,6},{8,9},{9,8},{10,11... | collective-permute-start | bytes 884744 | tf_op jit(solution)/shard_map/ppermute | solution.py:66
  253.0 14.2 %collective-permute-start.126 = (f32[2,2,384,96]{2,3,1,0:T(8,128)S(1)}, f32[2,2,384,96]{2,3,1,0:T(8,128)S(1)}, u32[]{:S(2)}, u32[]{:S(2)}) collective-permute-start(f32[2,2,384,96]{2,3,1,0:T(8,128)S(1)} %fusion.725), channel_id=1, source_target_pairs={{0,1},{1,0},{2,3},{3,2},{4,5},{5,4},{6,7},{7,6},{8,9},{9,8},{10,11... | collective-permute-start | bytes 1769480 | tf_op jit(solution)/shard_map/ppermute | solution.py:66
  266.0 16.3 %collective-permute-start.114 = (bf16[2,2,384,96]{2,3,1,0:T(8,128)(2,1)S(1)}, bf16[2,2,384,96]{2,3,1,0:T(8,128)(2,1)S(1)}, u32[]{:S(2)}, u32[]{:S(2)}) collective-permute-start(bf16[2,2,384,96]{2,3,1,0:T(8,128)(2,1)S(1)} %get-tuple-element.2819), channel_id=1, source_target_pairs={{0,2},{1,3},{2,0},{3,1},{4,6},{5,7},{6,4},{7,5},{8,10},{9,11},{10,... | collective-permute-start | bytes 884744 | tf_op jit(solution)/shard_map/ppermute | solution.py:66
  267.1 21.3 %collective-permute-start.136 = (f32[2,2,384,96]{2,3,1,0:T(8,128)S(1)}, f32[2,2,384,96]{2,3,1,0:T(8,128)S(1)}, u32[]{:S(2)}, u32[]{:S(2)}) collective-permute-start(f32[2,2,384,96]{2,3,1,0:T(8,128)S(1)} %fusion.734), channel_id=1, source_target_pairs={{0,1},{1,0},{2,3},{3,2},{4,5},{5,4},{6,7},{7,6},{8,9},{9,8},{10,11... | collective-permute-start | bytes 1769480 | tf_op jit(solution)/shard_map/ppermute | solution.py:66
  268.1 14.1 %collective-permute-start.127 = (bf16[2,2,384,96]{2,3,1,0:T(8,128)(2,1)S(1)}, bf16[2,2,384,96]{2,3,1,0:T(8,128)(2,1)S(1)}, u32[]{:S(2)}, u32[]{:S(2)}) collective-permute-start(bf16[2,2,384,96]{2,3,1,0:T(8,128)(2,1)S(1)} %get-tuple-element.2825), channel_id=1, source_target_pairs={{0,2},{1,3},{2,0},{3,1},{4,6},{5,7},{6,4},{7,5},{8,10},{9,11},{10,... | collective-permute-start | bytes 884744 | tf_op jit(solution)/shard_map/ppermute | solution.py:66
  271.0 16.0 %collective-permute-start.124 = (bf16[2,2,384,96]{2,3,1,0:T(8,128)(2,1)S(1)}, bf16[2,2,384,96]{2,3,1,0:T(8,128)(2,1)S(1)}, u32[]{:S(2)}, u32[]{:S(2)}) collective-permute-start(bf16[2,2,384,96]{2,3,1,0:T(8,128)(2,1)S(1)} %get-tuple-element.2823), channel_id=1, source_target_pairs={{0,2},{1,3},{2,0},{3,1},{4,6},{5,7},{6,4},{7,5},{8,10},{9,11},{10,... | collective-permute-start | bytes 884744 | tf_op jit(solution)/shard_map/ppermute | solution.py:66
  289.4 18.2 %collective-permute-start.125 = (bf16[2,2,384,96]{2,3,0,1:T(8,128)(2,1)S(1)}, bf16[2,2,384,96]{2,3,0,1:T(8,128)(2,1)S(1)}, u32[]{:S(2)}, u32[]{:S(2)}) collective-permute-start(bf16[2,2,384,96]{2,3,0,1:T(8,128)(2,1)S(1)} %get-tuple-element.2795), channel_id=1, source_target_pairs={{0,1},{1,0},{2,3},{3,2},{4,5},{5,4},{6,7},{7,6},{8,9},{9,8},{10,11... | collective-permute-start | bytes 884744 | tf_op jit(solution)/shard_map/ppermute | solution.py:66
  290.9 16.8 %collective-permute-start.128 = (bf16[2,2,384,96]{2,3,0,1:T(8,128)(2,1)S(1)}, bf16[2,2,384,96]{2,3,0,1:T(8,128)(2,1)S(1)}, u32[]{:S(2)}, u32[]{:S(2)}) collective-permute-start(bf16[2,2,384,96]{2,3,0,1:T(8,128)(2,1)S(1)} %get-tuple-element.2796), channel_id=1, source_target_pairs={{0,1},{1,0},{2,3},{3,2},{4,5},{5,4},{6,7},{7,6},{8,9},{9,8},{10,11... | collective-permute-start | bytes 884744 | tf_op jit(solution)/shard_map/ppermute | solution.py:66
  293.4 13.3 %collective-permute-start.134 = (bf16[2,2,384,96]{2,3,0,1:T(8,128)(2,1)S(1)}, bf16[2,2,384,96]{2,3,0,1:T(8,128)(2,1)S(1)}, u32[]{:S(2)}, u32[]{:S(2)}) collective-permute-start(bf16[2,2,384,96]{2,3,0,1:T(8,128)(2,1)S(1)} %get-tuple-element.2827), channel_id=1, source_target_pairs={{0,2},{1,3},{2,0},{3,1},{4,6},{5,7},{6,4},{7,5},{8,10},{9,11},{10,... | collective-permute-start | bytes 884744 | tf_op jit(solution)/shard_map/ppermute | solution.py:66
  351.0 48.8 %collective-permute-start.42 = (bf16[512,768]{1,0:T(8,128)(2,1)}, bf16[512,768]{1,0:T(8,128)(2,1)S(1)}, u32[]{:S(2)}, u32[]{:S(2)}) collective-permute-start(bf16[512,768]{1,0:T(8,128)(2,1)} %fusion.344), channel_id=1, source_target_pairs={{0,4},{1,5},{2,6},{3,7},{4,0},{5,1},{6,2},{7,3},{8,12},{9,13},{10,... | collective-permute-start | bytes 2359304 | tf_op jit(solution)/shard_map/cond/branch_6_fun/ppermute | solution.py:66
  359.4 42.0 %collective-permute-start.43 = (bf16[896,768]{1,0:T(8,128)(2,1)}, bf16[896,768]{1,0:T(8,128)(2,1)}, u32[]{:S(2)}, u32[]{:S(2)}) collective-permute-start(bf16[896,768]{1,0:T(8,128)(2,1)} %fusion.328), channel_id=1, source_target_pairs={{0,8},{1,9},{2,10},{3,11},{4,12},{5,13},{6,14},{7,15},{8,16},{9,17... | collective-permute-start | bytes 4128776 | tf_op jit(solution)/shard_map/cond/branch_6_fun/ppermute | solution.py:66
  368.1 112.6 %collective-permute-start.45 = (bf16[896,768]{1,0:T(8,128)(2,1)}, bf16[896,768]{1,0:T(8,128)(2,1)}, u32[]{:S(2)}, u32[]{:S(2)}) collective-permute-start(bf16[896,768]{1,0:T(8,128)(2,1)} %fusion.331), channel_id=1, source_target_pairs={{0,16},{1,17},{2,18},{3,19},{4,20},{5,21},{6,22},{7,23},{8,24},{9,... | collective-permute-start | bytes 4128776 | tf_op jit(solution)/shard_map/cond/branch_6_fun/ppermute | solution.py:66
  375.3 109.5 %collective-permute-start.47 = (bf16[896,768]{1,0:T(8,128)(2,1)}, bf16[896,768]{1,0:T(8,128)(2,1)}, u32[]{:S(2)}, u32[]{:S(2)}) collective-permute-start(bf16[896,768]{1,0:T(8,128)(2,1)} %fusion.334), channel_id=1, source_target_pairs={{0,24},{1,25},{2,26},{3,27},{4,28},{5,29},{6,30},{7,31},{8,0},{9,1... | collective-permute-start | bytes 4128776 | tf_op jit(solution)/shard_map/cond/branch_6_fun/ppermute | solution.py:66
  404.6 96.9 %collective-permute-start.44 = (bf16[512,768]{1,0:T(8,128)(2,1)}, bf16[512,768]{1,0:T(8,128)(2,1)}, u32[]{:S(2)}, u32[]{:S(2)}) collective-permute-start(bf16[512,768]{1,0:T(8,128)(2,1)} %fusion.350), channel_id=1, source_target_pairs={{0,4},{1,5},{2,6},{3,7},{4,0},{5,1},{6,2},{7,3},{8,12},{9,13},{10,... | collective-permute-start | bytes 2359304 | tf_op jit(solution)/shard_map/cond/branch_6_fun/ppermute | solution.py:66
  483.9 20.8 %collective-permute-start.46 = (bf16[512,768]{1,0:T(8,128)(2,1)}, bf16[512,768]{1,0:T(8,128)(2,1)}, u32[]{:S(2)}, u32[]{:S(2)}) collective-permute-start(bf16[512,768]{1,0:T(8,128)(2,1)} %fusion.351), channel_id=1, source_target_pairs={{0,4},{1,5},{2,6},{3,7},{4,0},{5,1},{6,2},{7,3},{8,12},{9,13},{10,... | collective-permute-start | bytes 2359304 | tf_op jit(solution)/shard_map/cond/branch_6_fun/ppermute | solution.py:66
  488.1 31.3 %collective-permute-start.48 = (bf16[512,768]{1,0:T(8,128)(2,1)}, bf16[512,768]{1,0:T(8,128)(2,1)}, u32[]{:S(2)}, u32[]{:S(2)}) collective-permute-start(bf16[512,768]{1,0:T(8,128)(2,1)} %fusion.352), channel_id=1, source_target_pairs={{0,4},{1,5},{2,6},{3,7},{4,0},{5,1},{6,2},{7,3},{8,12},{9,13},{10,... | collective-permute-start | bytes 2359304 | tf_op jit(solution)/shard_map/cond/branch_6_fun/ppermute | solution.py:66
  (80 other events, 797.7 us)
